TPU v7x, 256 devices: a whole 4x4x8 slice. The times are simulated.
256 devices in a mesh: dp: 16 (over z, core), expert: 16 (over x, y).
Axes of the slice: x: 4, y: 4, z: 8, core: 2. Of those that a mesh axis runs over, the one named last changes fastest.
Arguments:
- activations: bfloat16 [16384, 8, 768], P(('dp', 'expert')), may hold values from -6 to 6
- out_grad: bfloat16 [16384, 2048], P(('dp', 'expert')), may hold values from -0.796875 to 0.796875
- gate_weights: float32 [16384, 8], P(('dp', 'expert')), may hold values from 0.02 to 0.3
- routes: int32 [16384, 8], P(('dp', 'expert')), may hold values from 0 to 63, all different within a row; in each aligned block of 64 rows (0 to 63, 64 to 127, ...) at most 16 rows name the same one
- momentum: float32 [131072, 768], P(('expert', 'dp')), may hold values from -4 to 4
Outputs:
- update: bfloat16 [131072, 768], P(('expert', 'dp'))
- new_momentum: float32 [131072, 768], P(('expert', 'dp'))
Inputs may be any that keep to these rules, and one draw needn't show every extreme that they name: `routes`: each row names 8 different experts. Among the 64 rows of one device no expert is named by more than 16 rows, and in every draw some expert is named by exactly 16 rows of some device.
All inputs are finite; a program needn't handle non-finite values.
Results may differ from a plain program's by a relative error of at most 0.029.
Values may be sent and summed in bfloat16 or wider, within the bound.
A program may use at most 128 MiB of HBM per device.

v0:
```python
import math
import jax
import jax.numpy as jnp
from jax import lax
from jax.sharding import PartitionSpec as P

EXP_DEV = 4
NS_ITERS = 2
MOMENT = 0.95
COEFF_A = 3.4445
COEFF_B = -4.775
COEFF_C = 2.0315
EPSILON = 1e-07


def swapped(block, axis, apart):
    count = lax.axis_size(axis)
    route = []
    for low in range(count):
        high = low | 1 << apart
        if high != low and high < count:
            route += [(low, high), (high, low)]
    return lax.ppermute(block, axis, route)


def slot_table(routing, expert_total, capacity):
    tokens_here = routing.shape[0]
    slots_token = routing.shape[1]
    numbers = jnp.arange(expert_total, dtype=jnp.int32)
    matched = (routing[:, :, None] == numbers[None, None, :]).astype(jnp.int32)
    named_by = jnp.sum(matched, axis=1)
    position = jnp.sum(matched * jnp.arange(slots_token, dtype=jnp.int32)[None, :, None], axis=1)
    earlier = jnp.cumsum(named_by, axis=0) - named_by
    places = jnp.arange(capacity, dtype=jnp.int32)
    picked = ((named_by[:, :, None] == 1) & (earlier[:, :, None] == places[None, None, :])).astype(
        jnp.int32
    )
    pair_index = jnp.arange(tokens_here, dtype=jnp.int32)[:, None] * slots_token + position
    source = jnp.sum(picked * pair_index[:, :, None], axis=0)
    filled = jnp.sum(picked, axis=0) > 0
    return (source, filled)


def pack_slots(hidden_block, grad_block, gate_block, source, filled, slots_token):
    hidden_rows = hidden_block.reshape(-1, hidden_block.shape[-1])
    picked_rows = jnp.where(
        filled[..., None], jnp.take(hidden_rows, source, axis=0), jnp.zeros((), hidden_rows.dtype)
    )
    scales = jnp.where(filled, jnp.take(gate_block.reshape(-1), source), jnp.zeros((), jnp.float32))
    grad_rows = jnp.take(grad_block, source // slots_token, axis=0).astype(jnp.float32)
    weighted = (scales[..., None] * grad_rows).astype(jnp.bfloat16)
    return (picked_rows, weighted)


def newton_update(scaled, gram):
    square = jnp.dot(gram, gram, preferred_element_type=jnp.float32)
    poly = (COEFF_B * gram.astype(jnp.float32) + COEFF_C * square).astype(jnp.bfloat16)
    product = jnp.dot(scaled, poly, preferred_element_type=jnp.float32)
    return (COEFF_A * scaled.astype(jnp.float32) + product).astype(jnp.bfloat16)


def gram_of(scaled):
    return lax.dot_general(
        scaled, scaled, (((0,), (0,)), ((), ())), preferred_element_type=jnp.float32
    )


def body(activations, out_grad, gate_weights, routes, momentum):
    expert_count = lax.axis_size("expert")
    dp_count = lax.axis_size("dp")
    tokens_here = routes.shape[0]
    slots_token = routes.shape[1]
    expert_total = EXP_DEV * expert_count
    capacity = min(tokens_here, 2 * tokens_here * slots_token // expert_total)
    model_width = out_grad.shape[1]
    hidden_width = activations.shape[2]
    own_rows = momentum.shape[0]
    group_size = dp_count // EXP_DEV
    levels = group_size.bit_length() - 1
    source, filled = slot_table(routes, expert_total, capacity)
    source = (
        source.reshape(expert_count, EXP_DEV, capacity)
        .transpose(1, 0, 2)
        .reshape(EXP_DEV, expert_count * capacity)
    )
    filled = (
        filled.reshape(expert_count, EXP_DEV, capacity)
        .transpose(1, 0, 2)
        .reshape(EXP_DEV, expert_count * capacity)
    )
    hidden_send, weighted_send = pack_slots(
        activations, out_grad, gate_weights, source, filled, slots_token
    )
    hidden_got, weighted_got = (
        lax.all_to_all(hidden_send, "expert", split_axis=1, concat_axis=1, tiled=True),
        lax.all_to_all(weighted_send, "expert", split_axis=1, concat_axis=1, tiled=True),
    )

    def block_rows(block_index):
        begin_row = block_index * own_rows
        expert_local = begin_row // model_width
        column = begin_row % model_width
        hidden_expert = lax.dynamic_index_in_dim(hidden_got, expert_local, 0, keepdims=False)
        weighted_expert = lax.dynamic_index_in_dim(weighted_got, expert_local, 0, keepdims=False)
        columns = lax.dynamic_slice_in_dim(weighted_expert, column, own_rows, 1)
        return lax.dot_general(
            columns, hidden_expert, (((0,), (0,)), ((), ())), preferred_element_type=jnp.float32
        )

    blocks = lax.map(
        block_rows, jnp.arange(own_rows * lax.axis_size("dp") // own_rows, dtype=jnp.int32)
    )
    gradient = lax.psum_scatter(
        blocks.reshape(own_rows * lax.axis_size("dp"), hidden_width).astype(jnp.bfloat16),
        "dp",
        scatter_dimension=0,
        tiled=True,
    ).astype(jnp.float32)
    new_momentum = MOMENT * momentum + gradient
    ahead = gradient + MOMENT * new_momentum
    rank_dp = lax.axis_index("dp")
    part_index = rank_dp % group_size
    gathered = ahead
    for bit_index in range(levels):
        other = swapped(gathered.astype(jnp.bfloat16), "dp", bit_index).astype(gathered.dtype)
        upper = rank_dp // 2**bit_index % 2
        gathered = jnp.where(
            upper == 0, jnp.concatenate([gathered, other], 0), jnp.concatenate([other, gathered], 0)
        )
    norm_value = jnp.sqrt(jnp.sum(gathered * gathered))
    scaled_whole = (gathered / (norm_value + EPSILON)).astype(jnp.bfloat16)
    for turn_index in range(NS_ITERS):
        gram = gram_of(scaled_whole).astype(jnp.bfloat16)
        scaled_whole = newton_update(scaled_whole, gram)
    scaled = lax.dynamic_slice_in_dim(scaled_whole, part_index * own_rows, own_rows, 0)
    update = (math.sqrt(model_width) * scaled.astype(jnp.float32)).astype(jnp.bfloat16)
    return (update, new_momentum)


def solution(mesh):
    in_specs = (
        P(("dp", "expert"), None, None),
        P(("dp", "expert"), None),
        P(("dp", "expert"), None),
        P(("dp", "expert"), None),
        P(("expert", "dp"), None),
    )
    out_specs = (P(("expert", "dp"), None), P(("expert", "dp"), None))
    return jax.shard_map(body, mesh=mesh, in_specs=in_specs, out_specs=out_specs, check_vma=False)
```

profile of v0, /device:TPU:1, one launch (start us, length us, event | category | flops | bytes accessed | tf_op | source)
XLA Modules:
  0.0 348.5 jit_solution(1447675559522099637)
XLA Ops:
  7.2 0.8 copy.28
  9.1 0.8 copy.33
  10.0 6.9 %gather_fusion = f32[1024]{0:T(1024)S(1)} fusion(f32[512]{0:T(512)S(1)} %reshape.202, s32[1024]{0:T(1024)S(1)} %broadcast_clamp_fusion.1), kind=kCustom, calls=%fused_computation | custom fusion | bytes 12288 | tf_op jit(solution)/shard_map/jit(_take)/gather | solution.py:49
  16.9 4.0 %gather_fusion.2 = bf16[1024,768]{1,0:T(8,128)(2,1)S(1)} fusion(bf16[512,768]{1,0:T(8,128)(2,1)S(1)} %bitcast.45, s32[1024]{0:T(1024)S(1)} %broadcast_clamp_fusion.1), kind=kCustom, calls=%fused_computation.2 | custom fusion | bytes 3149824 | tf_op jit(solution)/shard_map/jit(_take)/gather | solution.py:47
  21.3 4.3 %fusion.6 = bf16[4,256,768]{2,0,1:T(4,128)(2,1)} fusion(bf16[4,256,768]{2,1,0:T(8,128)(2,1)S(1)} %bitcast.48, pred[4,256]{0,1:T(8,128)(4,1)S(1)} %copy.39, pred[4,256]{0,1:T(8,128)(4,1)S(1)} %copy.38), kind=kLoop, calls=%fused_computation.23 | loop fusion | flops 1572864 | bytes 3147776 | tf_op jit(solution)/shard_map/jit(_where)/select_n | solution.py:46
  25.6 7.6 %all-to-all-start.1 = ((bf16[4,256,768]{2,0,1:T(4,128)(2,1)}), bf16[4,256,768]{2,0,1:T(4,128)(2,1)S(1)}, u32[]{:S(2)}, u32[]{:S(2)}) async-start(bf16[4,256,768]{2,0,1:T(4,128)(2,1)} %fusion.6), calls=%async_computation.1 | async-start | bytes 3145728 | tf_op jit(solution)/shard_map/all_to_all | solution.py:95
  33.6 6.0 %gather_fusion.1 = bf16[1024,2048]{1,0:T(8,128)(2,1)} fusion(bf16[64,2048]{1,0:T(8,128)(2,1)S(1)} %copy-done.2, s32[1024]{0:T(1024)S(1)} %broadcast_clamp_fusion), kind=kCustom, calls=%fused_computation.1 | custom fusion | bytes 8392704 | tf_op jit(solution)/shard_map/jit(_take)/gather | solution.py:50
  39.5 7.7 %multiply_convert_fusion = bf16[4,256,2048]{2,0,1:T(4,128)(2,1)} fusion(bf16[4,256,2048]{2,1,0:T(8,128)(2,1)} %bitcast.46, f32[4,256]{0,1:T(8,128)S(1)} %copy.35, pred[4,256]{0,1:T(8,128)(4,1)S(1)} %copy.36), kind=kLoop, calls=%fused_computation.9 | loop fusion | flops 8388608 | bytes 8393728 | tf_op jit(solution)/shard_map/convert_element_type | solution.py:51
  47.3 6.5 %all-to-all-done.1 = bf16[4,256,768]{2,0,1:T(4,128)(2,1)S(1)} async-done(((bf16[4,256,768]{2,0,1:T(4,128)(2,1)}), bf16[4,256,768]{2,0,1:T(4,128)(2,1)S(1)}, u32[]{:S(2)}, u32[]{:S(2)}) %all-to-all-start.1) | async-done | bytes 1572896 | tf_op jit(solution)/shard_map/all_to_all | solution.py:95
  53.8 5.4 %all-to-all-start = ((bf16[4,256,2048]{2,0,1:T(4,128)(2,1)}), bf16[4,256,2048]{2,0,1:T(4,128)(2,1)}, u32[]{:S(2)}, u32[]{:S(2)}) async-start(bf16[4,256,2048]{2,0,1:T(4,128)(2,1)} %multiply_convert_fusion), calls=%async_computation | async-start | bytes 8388608 | tf_op jit(solution)/shard_map/all_to_all | solution.py:96
  59.5 47.0 %all-to-all-done = bf16[4,256,2048]{2,0,1:T(4,128)(2,1)} async-done(((bf16[4,256,2048]{2,0,1:T(4,128)(2,1)}), bf16[4,256,2048]{2,0,1:T(4,128)(2,1)}, u32[]{:S(2)}, u32[]{:S(2)}) %all-to-all-start) | async-done | bytes 4194336 | tf_op jit(solution)/shard_map/all_to_all | solution.py:96
  106.5 6.4 %copy.41 = bf16[4,256,2048]{2,1,0:T(8,128)(2,1)} copy(bf16[4,256,2048]{2,0,1:T(4,128)(2,1)} %all-to-all-done) | data formatting | bytes 8388608 | tf_op jit(solution)/shard_map/while | solution.py:110
  112.9 58.6 %while.13 = (s32[]{:T(128)}, bf16[16,512,768]{2,1,0:T(8,128)(2,1)}, s32[16]{0:T(128)S(1)}, bf16[4,256,2048]{2,1,0:T(8,128)(2,1)}, bf16[4,256,768]{2,1,0:T(8,128)...) while((s32[]{:T(128)}, bf16[16,512,768]{2,1,0:T(8,128)(2,1)}, ...), condition=%wide.region_6.7_spmd, body=%wide.region_5.6_spmd.sunk | while | flops 201326624 | bytes 2228700 | solution.py:110
  112.9 0.6 dynamic_slice.48
  114.2 2.4 bitcast_dynamic-update-slice_fusion.2
  116.6 0.6 dynamic_slice.48
  117.8 2.4 bitcast_dynamic-update-slice_fusion.2
  120.2 0.6 dynamic_slice.48
  121.5 2.4 bitcast_dynamic-update-slice_fusion.2
  125.2 2.4 bitcast_dynamic-update-slice_fusion.2
  128.8 2.4 bitcast_dynamic-update-slice_fusion.2
  132.4 2.4 bitcast_dynamic-update-slice_fusion.2
  136.1 2.4 bitcast_dynamic-update-slice_fusion.2
  139.7 2.4 bitcast_dynamic-update-slice_fusion.2
  143.4 2.4 bitcast_dynamic-update-slice_fusion.2
  147.0 2.4 bitcast_dynamic-update-slice_fusion.2
  150.7 2.4 bitcast_dynamic-update-slice_fusion.2
  154.4 2.4 bitcast_dynamic-update-slice_fusion.2
  158.1 2.4 bitcast_dynamic-update-slice_fusion.2
  161.8 2.4 bitcast_dynamic-update-slice_fusion.2
  165.4 2.4 bitcast_dynamic-update-slice_fusion.2
  169.1 2.4 bitcast_dynamic-update-slice_fusion.2
  171.5 86.8 %reduce-scatter.2.cloned.1.call-done = bf16[512,768]{1,0:T(8,128)(2,1)} async-done(((bf16[8192,768]{1,0:T(8,128)(2,1)}), bf16[512,768]{1,0:T(8,128)(2,1)}) %reduce-scatter.2.cloned.1.call-update) | async-done | bytes 786448 | tf_op jit(solution)/shard_map/reduce_scatter | solution.py:113
  258.3 2.8 fusion.20
  261.1 1.9 collective-permute-start
  263.1 2.1 collective-permute-done
  265.3 2.1 fusion.19
  267.4 35.7 %collective-permute-done.1 = bf16[1024,768]{1,0:T(8,128)(2,1)} collective-permute-done((bf16[1024,768]{1,0:T(8,128)(2,1)S(1)}, bf16[1024,768]{1,0:T(8,128)(2,1)}, u32[]{:S(2)}, u32[]{:S(2)}) %collective-permute-start.1) | collective-permute-done | bytes 1572896 | tf_op jit(solution)/shard_map/ppermute | solution.py:23
  303.1 1.6 convert_element_type.82
  304.8 2.2 multiply_reduce_fusion
  307.7 3.7 %divide_convert_fusion = bf16[2048,768]{1,0:T(8,128)(2,1)S(1)} fusion(f32[1024,768]{1,0:T(8,128)} %get-tuple-element.121, f32[1024,768]{1,0:T(8,128)S(1)} %convert_element_type.82, f32[]{:T(128)S(6)} %add.168, pred[]{:T(512)S(6)} %eq.50), kind=kLoop, calls=%fused_computation.12 | loop fusion | flops 7864320 | bytes 9437189 | tf_op jit(solution)/shard_map/convert_element_type | solution.py:131
  311.4 1.6 copy-done.4
  313.1 3.8 %convolution_convert_fusion.1 = bf16[768,768]{1,0:T(8,128)(2,1)} fusion(bf16[2048,768]{1,0:T(8,128)(2,1)S(1)} %divide_convert_fusion), kind=kOutput, calls=%fused_computation.26 | convolution fusion | flops 2416508928 | bytes 4325376 | tf_op jit(solution)/shard_map/dot_general | solution.py:63
  316.8 7.5 %add_convert_fusion = bf16[2048,768]{1,0:T(8,128)(2,1)S(1)} fusion(bf16[2048,768]{1,0:T(8,128)(2,1)} %copy-done.4, bf16[768,768]{1,0:T(8,128)(2,1)} %convolution_convert_fusion.1), kind=kOutput, calls=%fused_computation.11 | convolution fusion | flops 3331129344 | bytes 7471104 | tf_op jit(solution)/shard_map/dot_general | solution.py:58
  324.3 1.7 copy-done.6
  326.0 3.7 %convolution_convert_fusion = bf16[768,768]{1,0:T(8,128)(2,1)} fusion(bf16[2048,768]{1,0:T(8,128)(2,1)S(1)} %add_convert_fusion), kind=kOutput, calls=%fused_computation.25 | convolution fusion | flops 2416508928 | bytes 4325376 | tf_op jit(solution)/shard_map/dot_general | solution.py:63
  329.7 9.2 %fusion.7 = f32[2048,768]{1,0:T(8,128)} fusion(bf16[2048,768]{1,0:T(8,128)(2,1)} %copy-done.6, bf16[768,768]{1,0:T(8,128)(2,1)} %convolution_convert_fusion), kind=kOutput, calls=%fused_computation.27 | convolution fusion | flops 3324837888 | bytes 10616832 | tf_op jit(solution)/shard_map/dot_general | solution.py:58
  338.9 2.7 multiply_convert_fusion.1
  (60 shorter events, 9.8 us)
Async XLA Ops:
  7.2 9.8 %copy-start = (bf16[64,8,768]{2,1,0:T(8,128)(2,1)S(1)}, bf16[64,8,768]{2,1,0:T(8,128)(2,1)}, u32[]{:S(2)}) copy-start(bf16[64,8,768]{2,1,0:T(8,128)(2,1)} %param.7) | copy-start | bytes 2359300
  21.3 12.2 %copy-start.2 = (bf16[64,2048]{1,0:T(8,128)(2,1)S(1)}, bf16[64,2048]{1,0:T(8,128)(2,1)}, u32[]{:S(2)}) copy-start(bf16[64,2048]{1,0:T(8,128)(2,1)} %param.8) | copy-start | bytes 786436
  25.6 28.2 %all-to-all-start.1 = ((bf16[4,256,768]{2,0,1:T(4,128)(2,1)}), bf16[4,256,768]{2,0,1:T(4,128)(2,1)S(1)}, u32[]{:S(2)}, u32[]{:S(2)}) async-start(bf16[4,256,768]{2,0,1:T(4,128)(2,1)} %fusion.6), calls=%async_computation.1 | async-start | bytes 3145728 | tf_op jit(solution)/shard_map/all_to_all | solution.py:95
  53.8 52.7 %all-to-all-start = ((bf16[4,256,2048]{2,0,1:T(4,128)(2,1)}), bf16[4,256,2048]{2,0,1:T(4,128)(2,1)}, u32[]{:S(2)}, u32[]{:S(2)}) async-start(bf16[4,256,2048]{2,0,1:T(4,128)(2,1)} %multiply_convert_fusion), calls=%async_computation | async-start | bytes 8388608 | tf_op jit(solution)/shard_map/all_to_all | solution.py:96
  59.2 199.1 %reduce-scatter.2.cloned.1.call-start = ((), (), s32[]{:S(2)}) async-start(), calls=%async_computation.3 | async-start | bytes 13369344 | tf_op jit(solution)/shard_map/reduce_scatter | solution.py:113
  171.5 86.8 %copy-start.5 = (f32[512,768]{1,0:T(8,128)S(1)}, f32[512,768]{1,0:T(8,128)}, u32[]{:S(2)}) copy-start(f32[512,768]{1,0:T(8,128)} %param.11) | copy-start | bytes 4718596
  261.1 4.0 %collective-permute-start = (bf16[512,768]{1,0:T(8,128)(2,1)}, bf16[512,768]{1,0:T(8,128)(2,1)S(1)}, u32[]{:S(2)}, u32[]{:S(2)}) collective-permute-start(bf16[512,768]{1,0:T(8,128)(2,1)} %get-tuple-element.122), channel_id=1, source_target_pairs={{0,16},{16,0},{32,48},{48,32},{64,80},{80,64},{96,112},{112,96},{1... | collective-permute-start | bytes 2359304 | tf_op jit(solution)/shard_map/ppermute | solution.py:23
  267.4 35.7 %collective-permute-start.1 = (bf16[1024,768]{1,0:T(8,128)(2,1)S(1)}, bf16[1024,768]{1,0:T(8,128)(2,1)}, u32[]{:S(2)}, u32[]{:S(2)}) collective-permute-start(bf16[1024,768]{1,0:T(8,128)(2,1)S(1)} %get-tuple-element.120), channel_id=1, source_target_pairs={{0,32},{32,0},{16,48},{48,16},{64,96},{96,64},{80,112},{112,80},{1... | collective-permute-start | bytes 4718600 | tf_op jit(solution)/shard_map/ppermute | solution.py:23
  267.4 37.4 %copy-start.3 = (f32[1024,768]{1,0:T(8,128)S(1)}, f32[1024,768]{1,0:T(8,128)}, u32[]{:S(2)}) copy-start(f32[1024,768]{1,0:T(8,128)} %get-tuple-element.121) | copy-start | bytes 9437188
  311.4 1.7 copy-start.4
  324.3 1.7 copy-start.6
  329.7 11.9 %copy-start.1 = (bf16[64,8,768]{2,1,0:T(8,128)(2,1)S(1)}, bf16[64,8,768]{2,1,0:T(8,128)(2,1)}, u32[]{:S(2)}) copy-start(bf16[64,8,768]{2,1,0:T(8,128)(2,1)} %param.7) | copy-start | bytes 2359300
Sparse Core Ops, SparseCore 0:
  171.6 86.6 reduce-scatter.1
where the time goes:
time: 350 us; the launch traced here: 348 us
  waiting for transfers between devices  178 us (51%)
  matrix products  62.3 us (18%)
  local copies, waits for them, and re-layouts  39 us (11%)
  other arithmetic  28 us (8%)
  between operations  15 us (4%)
  starting transfers between devices  14.9 us (4%)
  loops' own time  11.1 us (3%)
    reduce_scatter x1, waiting for transfers between devices, body(): lax.psum_scatter(blocks.reshape(own_rows * lax.axis_size('dp'), hidden_wi...  86.8 us
    all_to_all x1, waiting for transfers between devices, body(): lax.all_to_all(weighted_send, 'expert', split_axis=1, concat_axis=1, tile...  47 us
    dot_general x16, matrix products, block_rows(): lax.dot_general(columns, hidden_expert, (((0,), (0,)), ((), ())), preferr...  38.2 us
    ppermute x2, waiting for transfers between devices, swapped(): return lax.ppermute(block, axis, route)  37.8 us
    dot_general x2, matrix products, newton_update(): product = jnp.dot(scaled, poly, preferred_element_type=jnp.float32)  16.7 us
    another operation x1, loops' own time, body(): lax.map(block_rows, jnp.arange(own_rows * lax.axis_size('dp') // own_rows...  11.1 us
    dynamic_slice x16, local copies, waits for them, and re-layouts, body(): lax.map(block_rows, jnp.arange(own_rows * lax.axis_size('dp') // own_rows...  9.32 us
    convert_element_type x1, other arithmetic, pack_slots(): weighted = (scales[..., None] * grad_rows).astype(jnp.bfloat16)  7.74 us
  transfers between devices with their start and end apart: 5, of which 5 were waited for; matrix products, arithmetic and copies ran while one was open for 4% of the time, Pallas kernels for 0%

commit v1 on v0

--- a/solution.py
+++ b/solution.py
@@ -92,7 +92,12 @@
         activations, out_grad, gate_weights, source, filled, slots_token
     )
     hidden_got, weighted_got = (
-        lax.all_to_all(hidden_send, "expert", split_axis=1, concat_axis=1, tiled=True),
+        jnp.concatenate(
+            lax.all_to_all(
+                jnp.stack(jnp.split(hidden_send, lax.axis_size("expert"), axis=1)), "expert", 0, 0
+            ),
+            axis=1,
+        ),
         lax.all_to_all(weighted_send, "expert", split_axis=1, concat_axis=1, tiled=True),
     )
 

time: 350 us -> 356 us (1.017)
  local copies, waits for them, and re-layouts: 39 us -> 48.9 us
  other arithmetic: 28 us -> 24.2 us
    unnamed x18 -> x33, local copies, waits for them, and re-layouts: 4.99 us -> 14.7 us
    select_n x1, other arithmetic: 4.26 us -> 0.45 us  [pack_slots(): jnp.where(filled[..., None], jnp.take(hidden_rows, source, axis=0), jnp.z...]
where the time goes in v1:
time: 356 us; the launch traced here: 355 us
  waiting for transfers between devices  178 us (50%)
  matrix products  62.3 us (18%)
  local copies, waits for them, and re-layouts  48.9 us (14%)
  other arithmetic  24.2 us (7%)
  starting transfers between devices  15.1 us (4%)
  between operations  15 us (4%)
  loops' own time  11.1 us (3%)
    reduce_scatter x1, waiting for transfers between devices, body(): lax.psum_scatter(blocks.reshape(own_rows * lax.axis_size('dp'), hidden_wi...  86.8 us
    all_to_all x1, waiting for transfers between devices, body(): lax.all_to_all(weighted_send, 'expert', split_axis=1, concat_axis=1, tile...  47.1 us
    dot_general x16, matrix products, block_rows(): lax.dot_general(columns, hidden_expert, (((0,), (0,)), ((), ())), preferr...  38.1 us
    ppermute x2, waiting for transfers between devices, swapped(): return lax.ppermute(block, axis, route)  37.8 us
    dot_general x2, matrix products, newton_update(): product = jnp.dot(scaled, poly, preferred_element_type=jnp.float32)  16.7 us
    unnamed x33, local copies, waits for them, and re-layouts  14.7 us
    another operation x1, loops' own time, body(): lax.map(block_rows, jnp.arange(own_rows * lax.axis_size('dp') // own_rows...  11.1 us
    dynamic_slice x16, local copies, waits for them, and re-layouts, body(): lax.map(block_rows, jnp.arange(own_rows * lax.axis_size('dp') // own_rows...  9.32 us
  transfers between devices with their start and end apart: 5, of which 5 were waited for; matrix products, arithmetic and copies ran while one was open for 4% of the time, Pallas kernels for 0%

profile of v1, /device:TPU:1, one launch (start us, length us, event | category | flops | bytes accessed | tf_op | source)
XLA Modules:
  0.0 354.7 jit_solution(17353037474297925907)
XLA Ops:
  7.2 0.8 copy.28
  8.9 0.8 copy.33
  9.8 6.9 %gather_fusion = f32[1024]{0:T(1024)S(1)} fusion(f32[512]{0:T(512)S(1)} %reshape.208, s32[1024]{0:T(1024)S(1)} %get-tuple-element.130), kind=kCustom, calls=%fused_computation | custom fusion | bytes 12288 | tf_op jit(solution)/shard_map/jit(_take)/gather | solution.py:49
  16.9 4.0 %gather_fusion.2 = bf16[1024,768]{1,0:T(8,128)(2,1)S(1)} fusion(bf16[512,768]{1,0:T(8,128)(2,1)S(1)} %bitcast.111, s32[1024]{0:T(1024)S(1)} %get-tuple-element.130), kind=kCustom, calls=%fused_computation.2 | custom fusion | bytes 3149824 | tf_op jit(solution)/shard_map/jit(_take)/gather | solution.py:47
  21.4 0.6 fusion.23
  22.1 0.6 fusion.22
  24.0 0.6 fusion.19
  28.5 0.6 fusion.12
  31.8 7.7 %all-to-all-start.1 = ((bf16[16,4,16,768]{3,2,1,0:T(8,128)(2,1)}), bf16[16,4,16,768]{3,2,1,0:T(8,128)(2,1)S(1)}, u32[]{:S(2)}, u32[]{:S(2)}) async-start(bf16[16,4,16,768]{3,2,1,0:T(8,128)(2,1)} %fusion.8), calls=%async_computation.1 | async-start | bytes 3145728 | tf_op jit(solution)/shard_map/all_to_all | solution.py:96
  39.9 6.0 %gather_fusion.1 = bf16[1024,2048]{1,0:T(8,128)(2,1)} fusion(bf16[64,2048]{1,0:T(8,128)(2,1)S(1)} %copy-done.2, s32[1024]{0:T(1024)S(1)} %get-tuple-element.129), kind=kCustom, calls=%fused_computation.1 | custom fusion | bytes 8392704 | tf_op jit(solution)/shard_map/jit(_take)/gather | solution.py:50
  45.9 7.7 %multiply_convert_fusion = bf16[4,256,2048]{2,0,1:T(4,128)(2,1)} fusion(bf16[4,256,2048]{2,1,0:T(8,128)(2,1)} %bitcast.112, f32[4,256]{0,1:T(8,128)S(1)} %copy.35, pred[4,256]{0,1:T(8,128)(4,1)S(1)} %copy.36), kind=kLoop, calls=%fused_computation.9 | loop fusion | flops 8388608 | bytes 8393728 | tf_op jit(solution)/shard_map/convert_element_type | solution.py:51
  53.6 6.5 %all-to-all-done.1 = bf16[16,4,16,768]{3,2,1,0:T(8,128)(2,1)S(1)} async-done(((bf16[16,4,16,768]{3,2,1,0:T(8,128)(2,1)}), bf16[16,4,16,768]{3,2,1,0:T(8,128)(2,1)S(1)}, u32[]{:S(2)}, u32[]{:S(2)}) %all-to-all-start.1) | async-done | bytes 1572896 | tf_op jit(solution)/shard_map/all_to_all | solution.py:96
  60.1 5.4 %all-to-all-start = ((bf16[4,256,2048]{2,0,1:T(4,128)(2,1)}), bf16[4,256,2048]{2,0,1:T(4,128)(2,1)}, u32[]{:S(2)}, u32[]{:S(2)}) async-start(bf16[4,256,2048]{2,0,1:T(4,128)(2,1)} %multiply_convert_fusion), calls=%async_computation | async-start | bytes 8388608 | tf_op jit(solution)/shard_map/all_to_all | solution.py:101
  65.7 47.1 %all-to-all-done = bf16[4,256,2048]{2,0,1:T(4,128)(2,1)} async-done(((bf16[4,256,2048]{2,0,1:T(4,128)(2,1)}), bf16[4,256,2048]{2,0,1:T(4,128)(2,1)}, u32[]{:S(2)}, u32[]{:S(2)}) %all-to-all-start) | async-done | bytes 4194336 | tf_op jit(solution)/shard_map/all_to_all | solution.py:101
  112.8 6.4 %copy.39 = bf16[4,256,2048]{2,1,0:T(8,128)(2,1)} copy(bf16[4,256,2048]{2,0,1:T(4,128)(2,1)} %all-to-all-done) | data formatting | bytes 8388608 | tf_op jit(solution)/shard_map/while | solution.py:115
  119.2 58.5 %while.13 = (s32[]{:T(128)}, bf16[16,512,768]{2,1,0:T(8,128)(2,1)}, s32[16]{0:T(128)S(1)}, bf16[4,256,2048]{2,1,0:T(8,128)(2,1)}, bf16[4,256,768]{2,1,0:T(8,128)...) while((s32[]{:T(128)}, bf16[16,512,768]{2,1,0:T(8,128)(2,1)}, ...), condition=%wide.region_6.7_spmd, body=%wide.region_5.6_spmd.sunk | while | flops 201326624 | bytes 2229200 | solution.py:115
  120.5 2.4 bitcast_dynamic-update-slice_fusion.2
  124.1 2.4 bitcast_dynamic-update-slice_fusion.2
  127.8 2.4 bitcast_dynamic-update-slice_fusion.2
  131.5 2.4 bitcast_dynamic-update-slice_fusion.2
  135.1 2.4 bitcast_dynamic-update-slice_fusion.2
  138.7 2.4 bitcast_dynamic-update-slice_fusion.2
  142.4 2.4 bitcast_dynamic-update-slice_fusion.2
  146.1 2.4 bitcast_dynamic-update-slice_fusion.2
  149.7 2.4 bitcast_dynamic-update-slice_fusion.2
  153.3 2.4 bitcast_dynamic-update-slice_fusion.2
  157.0 2.5 bitcast_dynamic-update-slice_fusion.2
  160.7 2.4 bitcast_dynamic-update-slice_fusion.2
  164.4 2.4 bitcast_dynamic-update-slice_fusion.2
  168.1 2.4 bitcast_dynamic-update-slice_fusion.2
  171.7 2.4 bitcast_dynamic-update-slice_fusion.2
  175.4 2.4 bitcast_dynamic-update-slice_fusion.2
  177.8 86.8 %reduce-scatter.2.cloned.1.call-done = bf16[512,768]{1,0:T(8,128)(2,1)} async-done(((bf16[8192,768]{1,0:T(8,128)(2,1)}), bf16[512,768]{1,0:T(8,128)(2,1)}) %reduce-scatter.2.cloned.1.call-update) | async-done | bytes 786448 | tf_op jit(solution)/shard_map/reduce_scatter | solution.py:118
  264.6 2.8 fusion.35
  267.4 1.9 collective-permute-start
  269.3 2.1 collective-permute-done
  271.6 2.1 fusion.34
  273.7 35.7 %collective-permute-done.1 = bf16[1024,768]{1,0:T(8,128)(2,1)} collective-permute-done((bf16[1024,768]{1,0:T(8,128)(2,1)S(1)}, bf16[1024,768]{1,0:T(8,128)(2,1)}, u32[]{:S(2)}, u32[]{:S(2)}) %collective-permute-start.1) | collective-permute-done | bytes 1572896 | tf_op jit(solution)/shard_map/ppermute | solution.py:23
  309.4 1.6 convert_element_type.82
  311.1 2.2 multiply_reduce_fusion
  314.0 3.6 %divide_convert_fusion = bf16[2048,768]{1,0:T(8,128)(2,1)S(1)} fusion(f32[1024,768]{1,0:T(8,128)} %get-tuple-element.121, f32[1024,768]{1,0:T(8,128)S(1)} %convert_element_type.82, f32[]{:T(128)S(6)} %add.168, pred[]{:T(512)S(6)} %eq.50), kind=kLoop, calls=%fused_computation.12 | loop fusion | flops 7864320 | bytes 9437189 | tf_op jit(solution)/shard_map/convert_element_type | solution.py:136
  317.7 1.6 copy-done.4
  319.3 3.8 %convolution_convert_fusion.1 = bf16[768,768]{1,0:T(8,128)(2,1)} fusion(bf16[2048,768]{1,0:T(8,128)(2,1)S(1)} %divide_convert_fusion), kind=kOutput, calls=%fused_computation.25 | convolution fusion | flops 2416508928 | bytes 4325376 | tf_op jit(solution)/shard_map/dot_general | solution.py:63
  323.1 7.5 %add_convert_fusion = bf16[2048,768]{1,0:T(8,128)(2,1)S(1)} fusion(bf16[2048,768]{1,0:T(8,128)(2,1)} %copy-done.4, bf16[768,768]{1,0:T(8,128)(2,1)} %convolution_convert_fusion.1), kind=kOutput, calls=%fused_computation.11 | convolution fusion | flops 3331129344 | bytes 7471104 | tf_op jit(solution)/shard_map/dot_general | solution.py:58
  330.6 1.7 copy-done.6
  332.3 3.7 %convolution_convert_fusion = bf16[768,768]{1,0:T(8,128)(2,1)} fusion(bf16[2048,768]{1,0:T(8,128)(2,1)S(1)} %add_convert_fusion), kind=kOutput, calls=%fused_computation.24 | convolution fusion | flops 2416508928 | bytes 4325376 | tf_op jit(solution)/shard_map/dot_general | solution.py:63
  335.9 9.2 %fusion.6 = f32[2048,768]{1,0:T(8,128)} fusion(bf16[2048,768]{1,0:T(8,128)(2,1)} %copy-done.6, bf16[768,768]{1,0:T(8,128)(2,1)} %convolution_convert_fusion), kind=kOutput, calls=%fused_computation.26 | convolution fusion | flops 3324837888 | bytes 10616832 | tf_op jit(solution)/shard_map/dot_general | solution.py:58
  345.1 2.7 multiply_convert_fusion.1
  (73 shorter events, 19.4 us)
Async XLA Ops:
  7.2 9.8 %copy-start = (bf16[64,8,768]{2,1,0:T(8,128)(2,1)S(1)}, bf16[64,8,768]{2,1,0:T(8,128)(2,1)}, u32[]{:S(2)}) copy-start(bf16[64,8,768]{2,1,0:T(8,128)(2,1)} %param.7) | copy-start | bytes 2359300
  31.8 8.1 %copy-start.2 = (bf16[64,2048]{1,0:T(8,128)(2,1)S(1)}, bf16[64,2048]{1,0:T(8,128)(2,1)}, u32[]{:S(2)}) copy-start(bf16[64,2048]{1,0:T(8,128)(2,1)} %param.8) | copy-start | bytes 786436
  31.8 28.3 %all-to-all-start.1 = ((bf16[16,4,16,768]{3,2,1,0:T(8,128)(2,1)}), bf16[16,4,16,768]{3,2,1,0:T(8,128)(2,1)S(1)}, u32[]{:S(2)}, u32[]{:S(2)}) async-start(bf16[16,4,16,768]{3,2,1,0:T(8,128)(2,1)} %fusion.8), calls=%async_computation.1 | async-start | bytes 3145728 | tf_op jit(solution)/shard_map/all_to_all | solution.py:96
  60.1 52.7 %all-to-all-start = ((bf16[4,256,2048]{2,0,1:T(4,128)(2,1)}), bf16[4,256,2048]{2,0,1:T(4,128)(2,1)}, u32[]{:S(2)}, u32[]{:S(2)}) async-start(bf16[4,256,2048]{2,0,1:T(4,128)(2,1)} %multiply_convert_fusion), calls=%async_computation | async-start | bytes 8388608 | tf_op jit(solution)/shard_map/all_to_all | solution.py:101
  65.5 199.0 %reduce-scatter.2.cloned.1.call-start = ((), (), s32[]{:S(2)}) async-start(), calls=%async_computation.3 | async-start | bytes 13369344 | tf_op jit(solution)/shard_map/reduce_scatter | solution.py:118
  177.7 86.8 %copy-start.5 = (f32[512,768]{1,0:T(8,128)S(1)}, f32[512,768]{1,0:T(8,128)}, u32[]{:S(2)}) copy-start(f32[512,768]{1,0:T(8,128)} %param.11) | copy-start | bytes 4718596
  267.4 4.0 %collective-permute-start = (bf16[512,768]{1,0:T(8,128)(2,1)}, bf16[512,768]{1,0:T(8,128)(2,1)S(1)}, u32[]{:S(2)}, u32[]{:S(2)}) collective-permute-start(bf16[512,768]{1,0:T(8,128)(2,1)} %get-tuple-element.122), channel_id=1, source_target_pairs={{0,16},{16,0},{32,48},{48,32},{64,80},{80,64},{96,112},{112,96},{1... | collective-permute-start | bytes 2359304 | tf_op jit(solution)/shard_map/ppermute | solution.py:23
  273.7 35.7 %collective-permute-start.1 = (bf16[1024,768]{1,0:T(8,128)(2,1)S(1)}, bf16[1024,768]{1,0:T(8,128)(2,1)}, u32[]{:S(2)}, u32[]{:S(2)}) collective-permute-start(bf16[1024,768]{1,0:T(8,128)(2,1)S(1)} %get-tuple-element.120), channel_id=1, source_target_pairs={{0,32},{32,0},{16,48},{48,16},{64,96},{96,64},{80,112},{112,80},{1... | collective-permute-start | bytes 4718600 | tf_op jit(solution)/shard_map/ppermute | solution.py:23
  273.7 37.4 %copy-start.3 = (f32[1024,768]{1,0:T(8,128)S(1)}, f32[1024,768]{1,0:T(8,128)}, u32[]{:S(2)}) copy-start(f32[1024,768]{1,0:T(8,128)} %get-tuple-element.121) | copy-start | bytes 9437188
  317.7 1.6 copy-start.4
  330.6 1.7 copy-start.6
  335.9 11.9 %copy-start.1 = (bf16[64,8,768]{2,1,0:T(8,128)(2,1)S(1)}, bf16[64,8,768]{2,1,0:T(8,128)(2,1)}, u32[]{:S(2)}) copy-start(bf16[64,8,768]{2,1,0:T(8,128)(2,1)} %param.7) | copy-start | bytes 2359300
Sparse Core Ops, SparseCore 0:
  177.9 86.6 reduce-scatter.1
